TPU v7x, 128 devices: a whole 4x4x4 slice. The times are simulated.
128 devices in a mesh: seq: 32 (over y, x_hi, z), head: 4 (over x_lo, core).
Axes of the slice: x: 4 (x_hi: 2, x_lo: 2; x = x_hi * 2 + x_lo), y: 4, z: 4, core: 2. Of those that a mesh axis runs over, the one named last changes fastest.
Arguments:
- mixer_input: bfloat16 [65536, 5120], P('seq', 'head'), may hold values from -6 to 6
- write_map: bfloat16 [65536, 128], P('seq', 'head'), may hold values from -0.5 to 0.5
- read_map: bfloat16 [65536, 128], P('seq', 'head'), may hold values from -6 to 6
- step_size: float32 [80, 65536], P('head', 'seq'), may hold values from 0 to 0.5
- log_decay: float32 [80, 65536], P('head', 'seq'), may hold values from -3 to 0
- skip_gain: float32 [80], P('head'), may hold values from 0.5 to 1.5
- level_table: float32 [9, 8], replicated, may hold values from 0.5 to 2
- level_index: int32 [9, 65536], P(None, 'seq'), may hold values from 0 to 7
Outputs:
- mixer_output: bfloat16 [65536, 5120], P('seq', 'head')
All inputs are finite; a program needn't handle non-finite values.
Results may differ from a plain program's by a relative error of at most 0.0043.
Values may be sent and summed in bfloat16 or wider, within the bound.
A program may use at most 256 MiB of HBM per device.

v0:
```python
import jax
import jax.numpy as jnp
from jax import lax
from jax.sharding import PartitionSpec as P

BLOCK = 256


def pick_row(source, where_at):
    return lax.dynamic_index_in_dim(source, where_at, 0, keepdims=False)


def tree_merge(lower_state, lower_total, upper_state, upper_total):
    merged = jnp.exp(upper_total)[..., None, None] * lower_state + upper_state
    return (merged, lower_total + upper_total)


def pair_merge(state_rows, total_rows):
    paired_state = state_rows.reshape((-1, 2) + state_rows.shape[1:])
    paired_total = total_rows.reshape((-1, 2) + total_rows.shape[1:])
    return tree_merge(
        paired_state[:, 0], paired_total[:, 0], paired_state[:, 1], paired_total[:, 1]
    )


def on_device(
    mixer_input, write_map, read_map, step_size, log_decay, skip_gain, level_table, level_index
):
    token_count = mixer_input.shape[0]
    head_count = log_decay.shape[0]
    head_width = mixer_input.shape[1] // head_count
    block_count = token_count // BLOCK
    local_bits = block_count.bit_length() - 1
    device_bits = lax.axis_size("seq").bit_length() - 1
    level_count = level_table.shape[0]
    my_rank = lax.axis_index("seq")
    write_rows, read_rows = (
        lax.all_gather(write_map, "head", axis=1, tiled=True),
        lax.all_gather(read_map, "head", axis=1, tiled=True),
    )
    state_width = write_rows.shape[1]
    level_weight = jnp.zeros(level_index.shape, jnp.float32)
    for entry in range(level_table.shape[1]):
        level_weight = level_weight + jnp.where(
            level_index == entry, level_table[:, entry : entry + 1], 0.0
        )
    decay_sum = jnp.cumsum(log_decay.reshape(head_count, block_count, BLOCK), axis=2).transpose(
        1, 0, 2
    )
    block_decay = decay_sum[:, :, -1]
    step_blocks = step_size.reshape(head_count, block_count, BLOCK).transpose(1, 0, 2)
    causal = jnp.arange(BLOCK)[:, None] >= jnp.arange(BLOCK)[None, :]

    def block_rows(block_index, source):
        return lax.dynamic_slice_in_dim(source, block_index * BLOCK, BLOCK, 0)

    def block_input(block_index):
        return block_rows(block_index, mixer_input).reshape(BLOCK, head_count, head_width)

    def intra_block(block_index):
        scores = lax.dot_general(
            block_rows(block_index, read_rows),
            block_rows(block_index, write_rows),
            (((1,), (1,)), ((), ())),
            preferred_element_type=jnp.float32,
        )
        sums_here = pick_row(decay_sum, block_index)
        gap = jnp.where(causal[None], sums_here[:, :, None] - sums_here[:, None, :], -jnp.inf)
        mixing = (scores[None] * jnp.exp(gap)).astype(jnp.bfloat16)
        inputs = (
            block_input(block_index) * pick_row(step_blocks, block_index).T[:, :, None]
        ).astype(jnp.bfloat16)
        return jnp.einsum("hts,shp->thp", mixing, inputs, preferred_element_type=jnp.float32)

    def state_block(block_index):
        sums_here = pick_row(decay_sum, block_index)
        factor = pick_row(step_blocks, block_index) * jnp.exp(sums_here[:, -1:] - sums_here)
        end_inputs = (block_input(block_index) * factor.T[:, :, None]).astype(jnp.bfloat16)
        return jnp.einsum(
            "sn,shp->hnp",
            block_rows(block_index, write_rows),
            end_inputs,
            preferred_element_type=jnp.float32,
        )

    block_ids = jnp.arange(block_count, dtype=jnp.int32)
    trees = [lax.map(state_block, block_ids)]
    totals = [block_decay]
    for bit_pos in range(local_bits):
        merged_state, merged_total = pair_merge(trees[-1], totals[-1])
        trees.append(merged_state)
        totals.append(merged_total)
    own_state = trees[-1][0]
    own_total = totals[-1][0]
    flags = []
    for section_bit in range(device_bits):
        flags.append((my_rank >> section_bit & 1).astype(jnp.float32))
    buckets = []
    bucket_totals = []
    every_state, every_total = (
        lax.all_gather(own_state[None], "seq", axis=0, tiled=True),
        lax.all_gather(own_total[None], "seq", axis=0, tiled=True),
    )
    for section_bit in range(device_bits):
        bucket_at = jnp.maximum((my_rank >> section_bit) - 1, 0)
        buckets.append(pick_row(every_state, bucket_at))
        bucket_totals.append(pick_row(every_total, bucket_at))
        if section_bit + 1 < device_bits:
            every_state, every_total = pair_merge(every_state, every_total)

    def read_block(block_index):
        running = jnp.zeros((head_count,), jnp.float32)
        states = []
        for bit_pos in range(local_bits):
            shifted = block_index >> bit_pos
            bit_flag = (shifted & 1).astype(jnp.float32)
            bucket_at = jnp.maximum(shifted - 1, 0)
            states.append(
                (bit_flag * jnp.exp(running))[:, None, None] * pick_row(trees[bit_pos], bucket_at)
            )
            running = running + bit_flag * pick_row(totals[bit_pos], bucket_at)
        for section_bit in range(device_bits):
            states.append(
                (flags[section_bit] * jnp.exp(running))[:, None, None] * buckets[section_bit]
            )
            running = running + flags[section_bit] * bucket_totals[section_bit]
        stacked = jnp.stack(states, axis=1).reshape(
            head_count, (level_count - 1) * state_width, head_width
        )
        weights_here = lax.dynamic_slice_in_dim(level_weight, block_index * BLOCK, BLOCK, 1)
        read_here = block_rows(block_index, read_rows).astype(jnp.float32)
        queries = (weights_here[1:].T[:, :, None] * read_here[:, None, :]).reshape(
            BLOCK, (level_count - 1) * state_width
        )
        inter_part = jnp.einsum(
            "tk,hkp->thp",
            queries,
            stacked,
            precision=lax.Precision.HIGHEST,
            preferred_element_type=jnp.float32,
        )
        intra_part = intra_block(block_index)
        result = (
            weights_here[0][:, None, None] * intra_part
            + jnp.exp(pick_row(decay_sum, block_index)).T[:, :, None] * inter_part
            + skip_gain[None, :, None] * block_input(block_index)
        )
        return result.astype(jnp.bfloat16)

    mixed = lax.map(read_block, block_ids)
    return mixed.reshape(token_count, head_count * head_width)


def solution(mesh):
    placed = (
        P("seq", "head"),
        P("seq", "head"),
        P("seq", "head"),
        P("head", "seq"),
        P("head", "seq"),
        P("head"),
        P(),
        P(None, "seq"),
    )
    return jax.shard_map(
        on_device, mesh=mesh, in_specs=placed, out_specs=P("seq", "head"), check_vma=False
    )
```

profile of v0, /device:TPU:24, one launch (start us, length us, event | category | flops | bytes accessed | tf_op | source)
XLA Modules:
  0.0 628.0 jit_solution(4445325200167561303)
XLA Ops:
  6.5 8.0 %copy.113 = bf16[2048,1280]{0,1:T(8,128)(2,1)} copy(bf16[2048,1280]{1,0:T(8,128)(2,1)} %param.12) | data formatting | bytes 10485760
  15.3 7.2 %all_gather.13 = bf16[2048,128]{0,1:T(8,128)(2,1)S(1)} all-gather(bf16[2048,32]{0,1:T(8,128)(2,1)S(1)} %copy-done.5), channel_id=1, replica_groups=mesh['seq'=32,'head'=4] {'head'}, dimensions={1}, use_global_device_ids=true | all-gather | bytes 655360 | tf_op jit(solution)/shard_map/all_gather | solution.py:38
  23.6 11.3 %reduce-window.6 = f32[20,8,2,128]{3,1,2,0:T(8,128)S(1)} reduce-window(f32[20,8,2,128]{3,1,2,0:T(8,128)S(1)} %copy.98, f32[]{:T(128)} %constant.170.clone.1), window={size=1x1x1x128 pad=0_0x0_0x0_0x127_0}, to_apply=%region_0.1 | reduce-window | flops 5201920 | bytes 327684 | tf_op jit(solution)/shard_map/reduce-window
  37.1 59.3 %while.24 = (s32[]{:T(128)}, f32[8,20,128,64]{2,3,1,0:T(8,128)}, s32[8]{0:T(128)S(1)}, bf16[2048,1280]{0,1:T(8,128)(2,1)}, f32[8,20,256]{2,0,1:T(8,128)}, /*inde...) while((s32[]{:T(128)}, f32[8,20,128,64]{2,3,1,0:T(8,128)}, ...), condition=%wide.region_3.4_spmd, body=%wide.region_2.3_spmd.sunk | while | flops 84879368 | bytes 2974169 | solution.py:87
  42.5 2.0 fusion.96
  49.9 2.0 fusion.96
  57.3 2.0 fusion.96
  64.7 2.1 fusion.96
  72.2 2.0 fusion.96
  79.6 2.0 fusion.96
  87.0 2.1 fusion.96
  94.4 2.0 fusion.96
  96.6 3.2 fusion.72
  101.4 83.6 %all-gather = f32[32,1,20]{2,1,0:T(1,128)S(1)} all-gather(f32[1,1,20]{2,1,0:T(1,128)S(1)} %get-tuple-element.858), channel_id=2, replica_groups=mesh['seq'=32,'head'=4] {'seq'}, dimensions={0}, use_global_device_ids=true | all-gather | bytes 2640 | tf_op jit(solution)/shard_map/all_gather | solution.py:102
  185.2 10.5 %all_gather.12 = bf16[2048,128]{0,1:T(8,128)(2,1)} all-gather(bf16[2048,32]{0,1:T(8,128)(2,1)S(1)} %copy-done.6), channel_id=1, replica_groups=mesh['seq'=32,'head'=4] {'head'}, dimensions={1}, use_global_device_ids=true | all-gather | bytes 655360 | tf_op jit(solution)/shard_map/all_gather | solution.py:39
  197.0 4.4 fusion.50
  202.2 84.8 %all-gather.3.cloned.1.call-done = f32[32,20,128,64]{2,3,1,0:T(8,128)} async-done(((f32[1,20,128,64]{2,3,1,0:T(8,128)}), f32[32,20,128,64]{2,3,1,0:T(8,128)}) %all-gather.3.cloned.1.call-update) | async-done | bytes 20971536 | tf_op jit(solution)/shard_map/all_gather | solution.py:101
  287.1 19.2 %fusion.69 = (f32[16,1,20,128,64]{3,4,2,1,0:T(8,128)S(1)}, f32[16,20,128,64]{2,3,1,0:T(8,128)}, f32[16,20,128,64]{2,3,1,0:T(8,128)}, f32[16,1,20,128,64]{3,4,2,1,0:T(8,128)}) fusion(f32[16,2,20,128,64]{3,4,2,1,0:T(8,128)} %bitcast.346), kind=kLoop, calls=%fused_computation.164 | loop fusion | bytes 62914560 | tf_op jit(solution)/shard_map/slice | solution.py:22
  306.3 9.0 %fusion.48 = f32[8,2,20,128,64]{3,4,2,1,0:T(8,128)} fusion(f32[8,2,20]{2,1,0:T(2,128)S(1)} %bitcast.365, f32[8,2,20,128,64]{3,4,2,1,0:T(8,128)} %bitcast.343, f32[8,2,20,128,64]{3,4,2,1,0:T(8,128)S(1)} %bitcast.342), kind=kLoop, calls=%fused_computation.88 | loop fusion | flops 5242880 | bytes 31458560 | tf_op jit(solution)/shard_map/add | solution.py:14
  315.3 12.8 %fusion.70 = (f32[8,1,20,128,64]{3,4,2,1,0:T(8,128)}, f32[8,20,128,64]{2,3,1,0:T(8,128)}, f32[8,20,128,64]{2,3,1,0:T(8,128)}, f32[8,1,20,128,64]{3,4,2,1,0:T(8,128)}) fusion(f32[8,2,20,128,64]{3,4,2,1,0:T(8,128)} %fusion.48), kind=kLoop, calls=%fused_computation.165 | loop fusion | bytes 31457280 | tf_op jit(solution)/shard_map/slice | solution.py:22
  328.1 4.6 fusion.49
  338.2 2.0 dynamic-slice_bitcast_fusion.1
  340.2 262.4 %while.25 = (s32[]{:T(128)}, bf16[8,256,20,64]{1,3,2,0:T(8,128)(2,1)}, s32[8]{0:T(128)S(1)}, f32[9,2048]{1,0:T(8,128)}, bf16[2048,1280]{0,1:T(8,128)(2,1)}, /*in...) while((s32[]{:T(128)}, ...), condition=%wide.region_5.6_spmd.clone, body=%wide.region_4.5_spmd.clone.sunk | while | flops 4221272576 | bytes 28544268 | solution.py:150
  352.5 2.0 fusion.103
  355.3 2.1 fusion.104
  357.4 2.1 fusion.106
  365.1 7.8 %fusion.111 = bf16[8,256,20,64]{1,3,2,0:T(8,128)(2,1)} fusion(bf16[8,256,20,64]{1,3,2,0:T(8,128)(2,1)} %get-tuple-element.1193, s32[]{:T(128)S(6)} %copy.171, bf16[256,20,64]{0,2,1:T(8,128)(2,1)S(1)} %bitcast.340, f32[256,20,64]{0,2,1:T(8,128)S(1)} %fusion.102, f32[20,8,128,64]{2,3,1,0:T(8,128)} %fusion.110, f32[20]{0:T(128)S(1)} %get-tuple-element.1259, ...), kind=kOutput, calls=%fused_computation.33.clone.1 | convolution fusion | flops 4028760064 | bytes 8024148 | tf_op jit(solution)/shard_map/while/body/eval_jaxpr/tk,hkp->thp/dot_general | solution.py:135
  382.6 2.0 bitcast_dynamic-update-slice_fusion.2
  385.3 2.0 fusion.103
  388.1 2.1 fusion.104
  390.2 2.1 fusion.106
  397.9 7.8 %fusion.111 = bf16[8,256,20,64]{1,3,2,0:T(8,128)(2,1)} fusion(bf16[8,256,20,64]{1,3,2,0:T(8,128)(2,1)} %get-tuple-element.1193, s32[]{:T(128)S(6)} %copy.171, bf16[256,20,64]{0,2,1:T(8,128)(2,1)S(1)} %bitcast.340, f32[256,20,64]{0,2,1:T(8,128)S(1)} %fusion.102, f32[20,8,128,64]{2,3,1,0:T(8,128)} %fusion.110, f32[20]{0:T(128)S(1)} %get-tuple-element.1259, ...), kind=kOutput, calls=%fused_computation.33.clone.1 | convolution fusion | flops 4028760064 | bytes 8024148 | tf_op jit(solution)/shard_map/while/body/eval_jaxpr/tk,hkp->thp/dot_general | solution.py:135
  415.4 2.0 bitcast_dynamic-update-slice_fusion.2
  418.1 2.0 fusion.103
  420.9 2.1 fusion.104
  423.0 2.1 fusion.106
  430.7 7.8 %fusion.111 = bf16[8,256,20,64]{1,3,2,0:T(8,128)(2,1)} fusion(bf16[8,256,20,64]{1,3,2,0:T(8,128)(2,1)} %get-tuple-element.1193, s32[]{:T(128)S(6)} %copy.171, bf16[256,20,64]{0,2,1:T(8,128)(2,1)S(1)} %bitcast.340, f32[256,20,64]{0,2,1:T(8,128)S(1)} %fusion.102, f32[20,8,128,64]{2,3,1,0:T(8,128)} %fusion.110, f32[20]{0:T(128)S(1)} %get-tuple-element.1259, ...), kind=kOutput, calls=%fused_computation.33.clone.1 | convolution fusion | flops 4028760064 | bytes 8024148 | tf_op jit(solution)/shard_map/while/body/eval_jaxpr/tk,hkp->thp/dot_general | solution.py:135
  448.2 2.0 bitcast_dynamic-update-slice_fusion.2
  450.9 2.0 fusion.103
  453.7 2.1 fusion.104
  455.8 2.1 fusion.106
  463.5 7.8 %fusion.111 = bf16[8,256,20,64]{1,3,2,0:T(8,128)(2,1)} fusion(bf16[8,256,20,64]{1,3,2,0:T(8,128)(2,1)} %get-tuple-element.1193, s32[]{:T(128)S(6)} %copy.171, bf16[256,20,64]{0,2,1:T(8,128)(2,1)S(1)} %bitcast.340, f32[256,20,64]{0,2,1:T(8,128)S(1)} %fusion.102, f32[20,8,128,64]{2,3,1,0:T(8,128)} %fusion.110, f32[20]{0:T(128)S(1)} %get-tuple-element.1259, ...), kind=kOutput, calls=%fused_computation.33.clone.1 | convolution fusion | flops 4028760064 | bytes 8024148 | tf_op jit(solution)/shard_map/while/body/eval_jaxpr/tk,hkp->thp/dot_general | solution.py:135
  481.0 2.0 bitcast_dynamic-update-slice_fusion.2
  483.7 2.0 fusion.103
  486.5 2.1 fusion.104
  488.6 2.1 fusion.106
  496.3 7.8 %fusion.111 = bf16[8,256,20,64]{1,3,2,0:T(8,128)(2,1)} fusion(bf16[8,256,20,64]{1,3,2,0:T(8,128)(2,1)} %get-tuple-element.1193, s32[]{:T(128)S(6)} %copy.171, bf16[256,20,64]{0,2,1:T(8,128)(2,1)S(1)} %bitcast.340, f32[256,20,64]{0,2,1:T(8,128)S(1)} %fusion.102, f32[20,8,128,64]{2,3,1,0:T(8,128)} %fusion.110, f32[20]{0:T(128)S(1)} %get-tuple-element.1259, ...), kind=kOutput, calls=%fused_computation.33.clone.1 | convolution fusion | flops 4028760064 | bytes 8024148 | tf_op jit(solution)/shard_map/while/body/eval_jaxpr/tk,hkp->thp/dot_general | solution.py:135
  513.8 2.0 bitcast_dynamic-update-slice_fusion.2
  516.5 2.0 fusion.103
  519.3 2.1 fusion.104
  521.4 2.1 fusion.106
  529.1 7.8 %fusion.111 = bf16[8,256,20,64]{1,3,2,0:T(8,128)(2,1)} fusion(bf16[8,256,20,64]{1,3,2,0:T(8,128)(2,1)} %get-tuple-element.1193, s32[]{:T(128)S(6)} %copy.171, bf16[256,20,64]{0,2,1:T(8,128)(2,1)S(1)} %bitcast.340, f32[256,20,64]{0,2,1:T(8,128)S(1)} %fusion.102, f32[20,8,128,64]{2,3,1,0:T(8,128)} %fusion.110, f32[20]{0:T(128)S(1)} %get-tuple-element.1259, ...), kind=kOutput, calls=%fused_computation.33.clone.1 | convolution fusion | flops 4028760064 | bytes 8024148 | tf_op jit(solution)/shard_map/while/body/eval_jaxpr/tk,hkp->thp/dot_general | solution.py:135
  546.6 2.0 bitcast_dynamic-update-slice_fusion.2
  549.3 2.0 fusion.103
  552.1 2.1 fusion.104
  554.2 2.1 fusion.106
  561.9 7.8 %fusion.111 = bf16[8,256,20,64]{1,3,2,0:T(8,128)(2,1)} fusion(bf16[8,256,20,64]{1,3,2,0:T(8,128)(2,1)} %get-tuple-element.1193, s32[]{:T(128)S(6)} %copy.171, bf16[256,20,64]{0,2,1:T(8,128)(2,1)S(1)} %bitcast.340, f32[256,20,64]{0,2,1:T(8,128)S(1)} %fusion.102, f32[20,8,128,64]{2,3,1,0:T(8,128)} %fusion.110, f32[20]{0:T(128)S(1)} %get-tuple-element.1259, ...), kind=kOutput, calls=%fused_computation.33.clone.1 | convolution fusion | flops 4028760064 | bytes 8024148 | tf_op jit(solution)/shard_map/while/body/eval_jaxpr/tk,hkp->thp/dot_general | solution.py:135
  582.1 2.0 fusion.103
  584.9 2.1 fusion.104
  587.0 2.1 fusion.106
  594.7 7.8 %fusion.111 = bf16[8,256,20,64]{1,3,2,0:T(8,128)(2,1)} fusion(bf16[8,256,20,64]{1,3,2,0:T(8,128)(2,1)} %get-tuple-element.1193, s32[]{:T(128)S(6)} %copy.171, bf16[256,20,64]{0,2,1:T(8,128)(2,1)S(1)} %bitcast.340, f32[256,20,64]{0,2,1:T(8,128)S(1)} %fusion.102, f32[20,8,128,64]{2,3,1,0:T(8,128)} %fusion.110, f32[20]{0:T(128)S(1)} %get-tuple-element.1259, ...), kind=kOutput, calls=%fused_computation.33.clone.1 | convolution fusion | flops 4028760064 | bytes 8024148 | tf_op jit(solution)/shard_map/while/body/eval_jaxpr/tk,hkp->thp/dot_general | solution.py:135
  602.6 6.2 copy.118
  608.7 4.6 copy.133
  613.3 7.9 %copy.119 = bf16[2048,1280]{1,0:T(8,128)(2,1)} copy(bf16[2048,1280]{0,1:T(8,128)(2,1)} %bitcast.348) | data formatting | bytes 10485760 | tf_op jit(solution)/shard_map/reshape | solution.py:151
  (339 shorter events, 136.3 us)
Async XLA Ops:
  6.5 280.5 %all-gather.3.cloned.1.call-start = ((), (), s32[]{:S(2)}) async-start(), calls=%async_computation | async-start | bytes 21626880 | tf_op jit(solution)/shard_map/all_gather | solution.py:101
  6.5 8.0 %copy-start.3 = (f32[20,2048]{1,0:T(8,128)S(1)}, f32[20,2048]{1,0:T(8,128)}, u32[]{:S(2)}) copy-start(f32[20,2048]{1,0:T(8,128)} %param.15) | copy-start | bytes 491524
  6.5 8.8 %copy-start.5 = (bf16[2048,32]{0,1:T(8,128)(2,1)S(1)}, bf16[2048,32]{0,1:T(8,128)(2,1)}, u32[]{:S(2)}) copy-start(bf16[2048,32]{0,1:T(8,128)(2,1)} %param.13) | copy-start | bytes 393220
  6.5 16.9 %copy-start.4 = (f32[20,2048]{1,0:T(8,128)S(1)}, f32[20,2048]{1,0:T(8,128)}, u32[]{:S(2)}) copy-start(f32[20,2048]{1,0:T(8,128)} %param.16) | copy-start | bytes 491524
  100.2 85.1 %copy-start.6 = (bf16[2048,32]{0,1:T(8,128)(2,1)S(1)}, bf16[2048,32]{0,1:T(8,128)(2,1)}, u32[]{:S(2)}) copy-start(bf16[2048,32]{0,1:T(8,128)(2,1)} %param.14) | copy-start | bytes 393220
  100.2 95.6 %copy-start.8 = (f32[9,8]{0,1:T(8,128)S(1)}, f32[9,8]{0,1:T(8,128)}, u32[]{:S(2)}) copy-start(f32[9,8]{0,1:T(8,128)} %param.18) | copy-start | bytes 868
  195.8 5.6 copy-start.7
  335.0 5.2 copy-start.2
  355.2 6.2 copy-start.1
  355.2 7.1 %copy-start = (f32[20,128,64]{1,2,0:T(8,128)S(1)}, f32[20,128,64]{1,2,0:T(8,128)}, u32[]{:S(2)}) copy-start(f32[20,128,64]{1,2,0:T(8,128)} %get-tuple-element.1258) | copy-start | bytes 1966084 | tf_op jit(solution)/shard_map/while
  388.0 6.2 copy-start.1
  388.0 7.1 %copy-start = (f32[20,128,64]{1,2,0:T(8,128)S(1)}, f32[20,128,64]{1,2,0:T(8,128)}, u32[]{:S(2)}) copy-start(f32[20,128,64]{1,2,0:T(8,128)} %get-tuple-element.1258) | copy-start | bytes 1966084 | tf_op jit(solution)/shard_map/while
  420.8 6.2 copy-start.1
  420.8 7.1 %copy-start = (f32[20,128,64]{1,2,0:T(8,128)S(1)}, f32[20,128,64]{1,2,0:T(8,128)}, u32[]{:S(2)}) copy-start(f32[20,128,64]{1,2,0:T(8,128)} %get-tuple-element.1258) | copy-start | bytes 1966084 | tf_op jit(solution)/shard_map/while
  453.6 6.2 copy-start.1
  453.6 7.1 %copy-start = (f32[20,128,64]{1,2,0:T(8,128)S(1)}, f32[20,128,64]{1,2,0:T(8,128)}, u32[]{:S(2)}) copy-start(f32[20,128,64]{1,2,0:T(8,128)} %get-tuple-element.1258) | copy-start | bytes 1966084 | tf_op jit(solution)/shard_map/while
  486.4 6.2 copy-start.1
  486.4 7.1 %copy-start = (f32[20,128,64]{1,2,0:T(8,128)S(1)}, f32[20,128,64]{1,2,0:T(8,128)}, u32[]{:S(2)}) copy-start(f32[20,128,64]{1,2,0:T(8,128)} %get-tuple-element.1258) | copy-start | bytes 1966084 | tf_op jit(solution)/shard_map/while
  519.2 6.2 copy-start.1
  519.2 7.1 %copy-start = (f32[20,128,64]{1,2,0:T(8,128)S(1)}, f32[20,128,64]{1,2,0:T(8,128)}, u32[]{:S(2)}) copy-start(f32[20,128,64]{1,2,0:T(8,128)} %get-tuple-element.1258) | copy-start | bytes 1966084 | tf_op jit(solution)/shard_map/while
  552.0 6.2 copy-start.1
  552.0 7.1 %copy-start = (f32[20,128,64]{1,2,0:T(8,128)S(1)}, f32[20,128,64]{1,2,0:T(8,128)}, u32[]{:S(2)}) copy-start(f32[20,128,64]{1,2,0:T(8,128)} %get-tuple-element.1258) | copy-start | bytes 1966084 | tf_op jit(solution)/shard_map/while
  584.8 6.2 copy-start.1
  584.8 7.1 %copy-start = (f32[20,128,64]{1,2,0:T(8,128)S(1)}, f32[20,128,64]{1,2,0:T(8,128)}, u32[]{:S(2)}) copy-start(f32[20,128,64]{1,2,0:T(8,128)} %get-tuple-element.1258) | copy-start | bytes 1966084 | tf_op jit(solution)/shard_map/while
Sparse Core Ops, SparseCore 0:
  101.5 185.5 all-gather.2
where the time goes:
time: 637 us; the launch traced here: 628 us
  local copies, waits for them, and re-layouts  136 us (21%)
  other arithmetic  135 us (21%)
  blocking collectives  101 us (16%)
  matrix products  99.1 us (16%)
  waiting for transfers between devices  84.9 us (13%)
  loops' own time  58 us (9%)
  between operations  13.7 us (2%)
    while x56, other arithmetic  88.6 us
    all_gather x1, waiting for transfers between devices, on_device(): lax.all_gather(own_state[None], 'seq', axis=0, tiled=True)  84.8 us
    all_gather x1, blocking collectives, on_device(): lax.all_gather(own_total[None], 'seq', axis=0, tiled=True)  83.6 us
    dot_general x8, matrix products, read_block(): jnp.einsum('tk,hkp->thp', queries, stacked, precision=lax.Precision.HIGHE...  62.5 us
    another operation x1, loops' own time, on_device(): mixed = lax.map(read_block, block_ids)  39.8 us
    slice x4, local copies, waits for them, and re-layouts, pair_merge(): paired_state[:, 1]  36.9 us
    dynamic_slice x32, local copies, waits for them, and re-layouts, block_rows(): return lax.dynamic_slice_in_dim(source, block_index * BLOCK, BLOCK, 0)  25.9 us
    add x8, other arithmetic, tree_merge(): merged = jnp.exp(upper_total)[..., None, None] * lower_state + upper_state  21 us
  transfers between devices with their start and end apart: 1, of which 1 were waited for; matrix products, arithmetic and copies ran while one was open for 1% of the time, Pallas kernels for 0%

commit v1 on v0

v1 whole, which is shorter than its diff:
```python
import math

import jax
import jax.numpy as jnp
import numpy as np
from jax import lax
from jax.experimental import pallas as pl
from jax.experimental.pallas import tpu as pltpu
from jax.sharding import PartitionSpec as P

SUB = 128
NSUB = 16
TOKENS = SUB * NSUB
HEADS = 20
WIDE = 256
CHUNKS = 5
STATE = 128
SHARE = 32
LEVELS = 9
TABLE = 8
LOG2E = math.log2(math.e)
MESH = pl.DeviceIdType.MESH
BF = jnp.bfloat16
F32 = jnp.float32

COL_MIX, COL_END, COL_OUT, COL_FAR, COL_LEVEL, COL_SUM = 0, 24, 48, 72, 96, 104
LEVEL_LANE = [COL_LEVEL + i for i in range(8)] + [20]
SPREAD_BASE = (COL_END, COL_OUT, COL_FAR, COL_SUM)


def range_rows():
    rows = {}

    def row(lo, hi):
        return rows.setdefault((lo, hi), len(rows))

    merge = {}
    for i in range(4):
        for k in range(NSUB >> (i + 1)):
            merge[i, k] = row((2 * k + 1) << i, (2 * k + 2) << i)
    scale = {}
    for j in range(NSUB):
        bits = [i for i in range(4) if j >> i & 1]
        for i in bits[1:]:
            scale[j, i] = row((j >> i) << i, j)
    total = row(0, NSUB)
    return rows, merge, scale, total


ROWS, MERGE, SCALE, TOTAL = range_rows()
SKIP_ROW = 63
LOCAL = [(j, i) for j in range(NSUB) for i in range(4) if j >> i & 1]
LOCAL_AT = {pair: n for n, pair in enumerate(LOCAL)}


def range_matrix():
    w = np.zeros((64, 128), np.float32)
    for (lo, hi), r in ROWS.items():
        for part in range(3):
            w[r, part * NSUB + lo : part * NSUB + hi] = 1.0
    return w


def dot(a, b):
    return jnp.dot(a, b, preferred_element_type=F32)


def split2(v):
    hi = v.astype(BF)
    return hi, (v - hi.astype(F32)).astype(BF)


def split3(v):
    hi = v.astype(BF)
    rest = v - hi.astype(F32)
    mid = rest.astype(BF)
    return hi, mid, (rest - mid.astype(F32)).astype(BF)


def kernel(
    x_hbm, b_own, c_own, step_in, decay_in, skip_in, table_in, index_in, ranges_in,
    out_hbm,
    x_s, b_t, c_t, ld_s, st_s, lw_s, tab_s, m_s, rv_s, colf, colhl, tots, tots3,
    rexp, spread, tree, loc, scm, qs, part, out_s, zbuf, xbuf, ybuf, rbuf,
    tz, tx, ty, secc, secw,
    bs, br, cs, cr, tzs, tzr, txs, txr, tys, tyr, zs, zr, xs, xr, ys, yr, ins, outs,
):
    seq = lax.axis_index("seq")
    me = lax.axis_index("head")
    z, xh, y = seq % 4, (seq // 4) % 2, seq // 8
    sib = me // 2 * 2 + (me + 1) % 2
    opp = (me + 2) % 4

    def at(z=z, xh=xh, y=y, h=me):
        return {"seq": (y * 2 + xh) * 4 + z, "head": h}

    def remote(src, dst, ssem, rsem, where):
        return pltpu.make_async_remote_copy(
            src_ref=src, dst_ref=dst, send_sem=ssem, recv_sem=rsem,
            device_id=where, device_id_type=MESH,
        )

    def cols(j):
        return pl.ds(pl.multiple_of(j * SUB, SUB), SUB)

    peers = [at(h=sib), at(h=opp)]
    peers += [at(z=(z + d) % 4) for d in (1, 2, 3)]
    peers += [at(xh=1 - xh)]
    peers += [at(y=(y + d) % 4) for d in (1, 2, 3)]
    barrier = pltpu.get_barrier_semaphore()
    for p in peers:
        pl.semaphore_signal(barrier, inc=1, device_id=p, device_id_type=MESH)

    def x_in(c):
        return pltpu.make_async_copy(
            x_hbm.at[:, pl.ds(pl.multiple_of(c * WIDE, WIDE), WIDE)], x_s.at[c], ins.at[c]
        )

    for c in range(CHUNKS):
        x_in(c).start()

    own_rows = pl.ds(pl.multiple_of(me * SHARE, SHARE), SHARE)
    opp_rows = pl.ds(pl.multiple_of(opp * SHARE, SHARE), SHARE)
    b_t[own_rows, :] = b_own[...]
    c_t[own_rows, :] = c_own[...]

    def share_copies(buf, ss, rs):
        own = buf.at[own_rows]
        far = buf.at[opp_rows]
        return (
            remote(own, own, ss.at[0], rs.at[0], at(h=opp)),
            remote(own, own, ss.at[1], rs.at[1], at(h=sib)),
            remote(far, far, ss.at[2], rs.at[2], at(h=sib)),
        )

    b_copies = share_copies(b_t, bs, br)
    c_copies = share_copies(c_t, cs, cr)
    pl.semaphore_wait(barrier, len(peers))
    for k in (0, 1):
        b_copies[k].start()
    for k in (0, 1):
        c_copies[k].start()

    ld_s[...] = jnp.zeros_like(ld_s)
    st_s[...] = jnp.zeros_like(st_s)
    ld_s[0:HEADS, :] = decay_in[...]
    st_s[0:HEADS, :] = step_in[...]
    tab_s[...] = jnp.zeros_like(tab_s)
    tab_s[:, 0:LEVELS] = table_in[...]
    tab_t = tab_s[...].T
    lw_s[...] = jnp.ones_like(lw_s)
    weight = jnp.zeros((LEVELS, TOKENS), F32)
    index = index_in[...]
    for e in range(TABLE):
        weight = weight + jnp.where(index == e, tab_t[0:LEVELS, e : e + 1], 0.0)
    lw_s[0:LEVELS, :] = weight

    lanes3 = lax.broadcasted_iota(jnp.int32, (3 * SUB, SUB), 1)
    rows3 = lax.broadcasted_iota(jnp.int32, (3 * SUB, SUB), 0) & (SUB - 1)
    upper = jnp.where(rows3 <= lanes3, 1.0, 0.0).astype(BF)

    def prepare(j, off):
        here = cols(j)
        hi, mid, lo = split3(ld_s[:, here])
        d = dot(jnp.concatenate([hi, mid, lo], axis=1), upper)[0:24]
        total = jnp.broadcast_to(d[:, SUB - 1 : SUB], (24, SUB))
        log_step = jnp.log(st_s[0:24, here]) * LOG2E
        lw = lw_s[:, here]
        d2 = d * LOG2E
        rv = d2 - log_step
        for c in range(CHUNKS):
            rv_s[c, 0:4, here] = rv[4 * c : 4 * c + 4]
        m_s[0:24, :] = d2 + jnp.log(lw[0:1]) * LOG2E
        m_s[20:21, :] = lw[8:9]
        m_s[COL_END : COL_END + 24, :] = jnp.exp2((total - d) * LOG2E + log_step)
        m_s[COL_OUT : COL_OUT + 24, :] = jnp.exp2(d2)
        m_s[COL_FAR : COL_FAR + 24, :] = jnp.exp2((d + off) * LOG2E)
        m_s[COL_LEVEL : COL_LEVEL + 8, :] = lw[0:8]
        m_s[COL_SUM : COL_SUM + 24, :] = d
        mt = m_s[...].T
        colf[here, :] = mt
        hi2, lo2 = split2(mt)
        colhl[here, 0:SUB] = hi2
        colhl[here, SUB : 2 * SUB] = lo2
        tots[pl.ds(j, 1), :] = mt[SUB - 1 : SUB, :]
        return off + total

    lax.fori_loop(0, NSUB, prepare, jnp.zeros((24, SUB), F32))

    k_at = lax.broadcasted_iota(jnp.int32, (2 * SUB, WIDE), 0) & (SUB - 1)
    head_at = k_at - (lax.broadcasted_iota(jnp.int32, (2 * SUB, WIDE), 1) >> 6)

    def build(c, carry):
        for g, base in enumerate(SPREAD_BASE):
            spread[g, c] = jnp.where(head_at == base + 4 * c, 1.0, 0.0).astype(BF)
        return carry

    lax.fori_loop(0, CHUNKS, build, 0)

    tots3[...] = jnp.zeros_like(tots3)
    for n, piece in enumerate(split3(tots[...])):
        tots3[n * NSUB : (n + 1) * NSUB, :] = piece
    range_log = dot(ranges_in[...], tots3[...])
    lane_at = lax.broadcasted_iota(jnp.int32, (64, SUB), 1)
    range_log = jnp.where(lane_at >= COL_SUM, range_log, 0.0)
    own_total = jnp.broadcast_to(range_log[TOTAL : TOTAL + 1], (8, SUB))
    tz[z] = own_total

    def tz_copy(d):
        return remote(tz.at[z], tz.at[z], tzs.at[d - 1], tzr.at[d - 1], at(z=(z + d) % 4))

    def tz_arrival(d):
        k = (z - d) % 4
        return remote(tz.at[k], tz.at[k], tzs.at[d - 1], tzr.at[d - 1], at(z=k))

    for d in (1, 2, 3):
        tz_copy(d).start()

    tab_s[...] = jnp.zeros_like(tab_s)
    tab_s[0:1, 0:HEADS] = skip_in[...]
    skip_row = pltpu.roll(tab_s[...], COL_SUM, 1)[0:1]
    row_at = lax.broadcasted_iota(jnp.int32, (64, SUB), 0)
    factor = jnp.where(row_at == SKIP_ROW, skip_row, jnp.exp(range_log))
    factor = jnp.concatenate(split2(factor), axis=1)

    def spread_rows(c, carry):
        rexp[c] = dot(factor, spread[3, c])
        return carry

    lax.fori_loop(0, CHUNKS, spread_rows, 0)

    b_copies[0].wait_recv()
    b_copies[2].start()
    c_copies[0].wait_recv()
    c_copies[2].start()
    b_copies[1].wait_recv()
    b_copies[2].wait_recv()

    for d in (1, 2, 3):
        tz_arrival(d).wait_recv()
    far_t = [tz[k, 0:1] for k in range(4)]
    tx[xh] = jnp.broadcast_to(far_t[0] + far_t[1] + far_t[2] + far_t[3], (8, SUB))
    tx_copy = remote(tx.at[xh], tx.at[xh], txs, txr, at(xh=1 - xh))
    tx_copy.start()

    def z_copy(c, d):
        return remote(
            zbuf.at[c, z], zbuf.at[c, z], zs.at[c, d - 1], zr.at[c, d - 1], at(z=(z + d) % 4)
        )

    def z_arrival(c, d):
        k = (z - d) % 4
        return remote(zbuf.at[c, k], zbuf.at[c, k], zs.at[c, d - 1], zr.at[c, d - 1], at(z=k))

    first = {0: 0, 1: 16, 2: 24, 3: 28}

    def states(c, carry):
        x_in(c).wait()

        def one(j, carry):
            here = cols(j)
            end = dot(colhl[here, :], spread[0, c])
            scaled = (x_s[c, here, :].astype(F32) * end).astype(BF)
            tree[j] = dot(b_t[:, here], scaled)
            return carry

        lax.fori_loop(0, NSUB, one, 0)
        for i in range(4):
            for k in range(NSUB >> (i + 1)):
                r = MERGE[i, k]
                merged = (
                    rexp[c, r : r + 1, :] * tree[first[i] + 2 * k] + tree[first[i] + 2 * k + 1]
                )
                if i < 3:
                    tree[first[i + 1] + k] = merged
                else:
                    zbuf[c, z] = merged.astype(BF)
        for d in (1, 2, 3):
            z_copy(c, d).start()
        for (j, i), n in LOCAL_AT.items():
            value = tree[first[i] + (j >> i) - 1]
            if (j, i) in SCALE:
                r = SCALE[j, i]
                value = rexp[c, r : r + 1, :] * value
            loc[c, n * STATE : (n + 1) * STATE, :] = value.astype(BF)
        return carry

    lax.fori_loop(0, CHUNKS, states, 0)

    tx_copy.wait_recv()
    ty[y] = jnp.broadcast_to(tx[0, 0:1] + tx[1, 0:1], (8, SUB))

    def ty_copy(d):
        return remote(ty.at[y], ty.at[y], tys.at[d - 1], tyr.at[d - 1], at(y=(y + d) % 4))

    def ty_arrival(d):
        k = (y - d) % 4
        return remote(ty.at[k], ty.at[k], tys.at[d - 1], tyr.at[d - 1], at(y=k))

    for d in (1, 2, 3):
        ty_copy(d).start()

    c_copies[1].wait_recv()
    c_copies[2].wait_recv()
    causal = lax.broadcasted_iota(jnp.int32, (SUB, SUB), 0) >= lax.broadcasted_iota(
        jnp.int32, (SUB, SUB), 1
    )

    def queries(j, carry):
        here = cols(j)
        c_rows = c_t[:, here].astype(F32).T
        scm[j] = jnp.where(causal, dot(c_rows.astype(BF), b_t[:, here]), 0.0)
        tile = colf[here, :]
        for i, lane in enumerate(LEVEL_LANE):
            qs[here, i * STATE : (i + 1) * STATE] = (tile[:, lane : lane + 1] * c_rows).astype(BF)
        return carry

    lax.fori_loop(0, NSUB, queries, 0)

    for d in (1, 2, 3):
        ty_arrival(d).wait_recv()

    t0, t1, t2, t3 = far_t
    u0, u1 = tx[0, 0:1], tx[1, 0:1]
    v1, v2 = ty[1, 0:1], ty[2, 0:1]

    def only(flag, row):
        return jnp.where(flag, row, 0.0)

    run2 = only(z > 0, t0) + only(z > 1, t1) + only(z > 2, t2)
    run3 = run2 + only(xh == 1, u0)
    run4 = run3 + only(y == 3, v2)
    low_run = only(z == 3, t2)
    upper_z, upper_y = z >= 2, y >= 2
    weights = [
        jnp.exp(t1 + t2 + t3),
        jnp.exp(t2 + t3),
        jnp.exp(t3),
        only(upper_z, jnp.exp(t1 + low_run)),
        only(upper_z, jnp.exp(low_run)),
        only(xh == 1, jnp.exp(run2)),
        jnp.exp(u1),
        jnp.exp(run3),
        jnp.exp(v1 + run4),
        jnp.exp(run4),
    ]
    secc[...] = jnp.zeros_like(secc)
    for n, w in enumerate(weights):
        secc[n : n + 1, :] = w
    compact = jnp.concatenate(split2(secc[...]), axis=1)

    def spread_weights(c, carry):
        secw[c] = dot(compact, spread[3, c])
        return carry

    lax.fori_loop(0, CHUNKS, spread_weights, 0)

    def x_copy(c):
        return remote(xbuf.at[c, xh], xbuf.at[c, xh], xs.at[c], xr.at[c], at(xh=1 - xh))

    def x_arrival(c):
        k = 1 - xh
        return remote(xbuf.at[c, k], xbuf.at[c, k], xs.at[c], xr.at[c], at(xh=k))

    def y_copy(c, d):
        return remote(
            ybuf.at[c, y], ybuf.at[c, y], ys.at[c, d - 1], yr.at[c, d - 1], at(y=(y + d) % 4)
        )

    def y_arrival(c, d):
        k = (y - d) % 4
        return remote(ybuf.at[c, k], ybuf.at[c, k], ys.at[c, d - 1], yr.at[c, d - 1], at(y=k))

    def after_z(c):
        for d in (1, 2, 3):
            z_arrival(c, d).wait_recv()
        w = [secw[c, n : n + 1, :] for n in range(5)]
        s = [zbuf[c, k].astype(F32) for k in range(4)]
        xbuf[c, xh] = (w[0] * s[0] + w[1] * s[1] + (w[2] * s[2] + s[3])).astype(BF)
        x_copy(c).start()
        rbuf[c, 0:STATE, :] = jnp.where(
            z % 2 == 1, zbuf[c, jnp.maximum(z - 1, 0)].astype(F32), 0.0
        ).astype(BF)
        rbuf[c, STATE : 2 * STATE, :] = (w[3] * s[0] + w[4] * s[1]).astype(BF)

    def after_x(c):
        x_arrival(c).wait_recv()
        s = [xbuf[c, k].astype(F32) for k in range(2)]
        ybuf[c, y] = (secw[c, 6:7, :] * s[0] + s[1]).astype(BF)
        for d in (1, 2, 3):

            @pl.when(y + d < 4)
            def _():
                y_copy(c, d).start()

        rbuf[c, 2 * STATE : 3 * STATE, :] = (secw[c, 5:6, :] * s[0]).astype(BF)

    def after_y(c):
        for d in (1, 2, 3):

            @pl.when(y >= d)
            def _():
                y_arrival(c, d).wait_recv()

        near = secw[c, 7:8, :] * ybuf[c, jnp.maximum(y - 1, 0)].astype(F32)
        rbuf[c, 3 * STATE : 4 * STATE, :] = jnp.where(y % 2 == 1, near, 0.0).astype(BF)
        wide = secw[c, 8:9, :] * ybuf[c, 0].astype(F32) + secw[c, 9:10, :] * ybuf[c, 1].astype(F32)
        rbuf[c, 4 * STATE : 5 * STATE, :] = jnp.where(upper_y, wide, 0.0).astype(BF)

    low_half = lax.broadcasted_iota(jnp.int32, (SUB, SUB), 1) < 64

    def local_part(c):
        turn = lax.rem(SUB - 4 * c, SUB)
        skip = rexp[c, SKIP_ROW : SKIP_ROW + 1, :]
        for j in range(NSUB):
            here = pl.ds(j * SUB, SUB)
            tile = pltpu.roll(colf[here, :], turn, 1)
            masked = scm[j]
            xt = x_s[c, here, :]
            xf = xt.astype(F32)
            halves = []
            for pair in range(2):
                mixes = []
                for k in (2 * pair, 2 * pair + 1):
                    gap = tile[:, k : k + 1] - rv_s[c, k : k + 1, here]
                    mixes.append((masked * jnp.exp2(jnp.minimum(gap, 64.0))).astype(BF))
                xp = xf[:, pair * SUB : (pair + 1) * SUB]
                both = jnp.concatenate(
                    [
                        jnp.where(low_half, xp, 0.0).astype(BF),
                        jnp.where(low_half, 0.0, xp).astype(BF),
                    ],
                    axis=0,
                )
                halves.append(dot(jnp.concatenate(mixes, axis=1), both))
            result = jnp.concatenate(halves, axis=1) + skip * xf
            bits = [i for i in range(4) if j >> i & 1]
            if bits:
                q = jnp.concatenate([qs[here, i * STATE : (i + 1) * STATE] for i in bits], axis=1)
                lo = LOCAL_AT[j, bits[0]] * STATE
                near = dot(q, loc[c, lo : lo + len(bits) * STATE, :])
                result = result + dot(colhl[here, :], spread[1, c]) * near
            part[c, here, :] = result

    def out_copy(c):
        return pltpu.make_async_copy(
            out_s.at[c], out_hbm.at[:, pl.ds(pl.multiple_of(c * WIDE, WIDE), WIDE)], outs.at[c]
        )

    def finish(c):
        def one(j, carry):
            here = pl.ds(pl.multiple_of(j * 256, 256), 256)
            far = dot(qs[here, 4 * STATE : 9 * STATE], rbuf[c])
            result = part[c, here, :] + dot(colhl[here, :], spread[2, c]) * far
            out_s[c, here, :] = result.astype(BF)
            return carry

        lax.fori_loop(0, TOKENS // 256, one, 0)
        out_copy(c).start()

    def step(i, carry):
        @pl.when(jnp.logical_and(i >= 1, i < 1 + CHUNKS))
        def _():
            after_z(i - 1)

        @pl.when(jnp.logical_and(i >= 3, i < 3 + CHUNKS))
        def _():
            after_x(i - 3)

        @pl.when(i >= 5)
        def _():
            after_y(i - 5)
            finish(i - 5)

        @pl.when(i < CHUNKS)
        def _():
            local_part(i)

        return carry

    lax.fori_loop(0, 5 + CHUNKS, step, 0)

    for copies in (b_copies, c_copies):
        for copy in copies:
            copy.wait_send()
    tx_copy.wait_send()
    for d in (1, 2, 3):
        tz_copy(d).wait_send()
        ty_copy(d).wait_send()

    def drain(c, carry):
        for d in (1, 2, 3):
            z_copy(c, d).wait_send()

            @pl.when(y + d < 4)
            def _():
                y_copy(c, d).wait_send()

        x_copy(c).wait_send()
        out_copy(c).wait()
        return carry

    lax.fori_loop(0, CHUNKS, drain, 0)


def on_device(
    mixer_input, write_map, read_map, step_size, log_decay, skip_gain, level_table, level_index
):
    vmem, hbm = pl.BlockSpec(memory_space=pltpu.VMEM), pl.BlockSpec(memory_space=pl.ANY)
    dma = pltpu.SemaphoreType.DMA
    columns = HEADS * 64
    return pl.pallas_call(
        kernel,
        out_shape=jax.ShapeDtypeStruct((TOKENS, columns), BF),
        in_specs=[hbm] + [vmem] * 8,
        out_specs=hbm,
        scratch_shapes=[
            pltpu.VMEM((CHUNKS, TOKENS, WIDE), BF),
            pltpu.VMEM((STATE, TOKENS), BF),
            pltpu.VMEM((STATE, TOKENS), BF),
            pltpu.VMEM((32, TOKENS), F32),
            pltpu.VMEM((32, TOKENS), F32),
            pltpu.VMEM((16, TOKENS), F32),
            pltpu.VMEM((8, SUB), F32),
            pltpu.VMEM((SUB, SUB), F32),
            pltpu.VMEM((CHUNKS, 8, TOKENS), F32),
            pltpu.VMEM((TOKENS, SUB), F32),
            pltpu.VMEM((TOKENS, 2 * SUB), BF),
            pltpu.VMEM((NSUB, SUB), F32),
            pltpu.VMEM((SUB, SUB), BF),
            pltpu.VMEM((CHUNKS, 64, WIDE), F32),
            pltpu.VMEM((4, CHUNKS, 2 * SUB, WIDE), BF),
            pltpu.VMEM((30, STATE, WIDE), F32),
            pltpu.VMEM((CHUNKS, len(LOCAL) * STATE, WIDE), BF),
            pltpu.VMEM((NSUB, SUB, SUB), F32),
            pltpu.VMEM((TOKENS, LEVELS * STATE), BF),
            pltpu.VMEM((CHUNKS, TOKENS, WIDE), F32),
            pltpu.VMEM((CHUNKS, TOKENS, WIDE), BF),
            pltpu.VMEM((CHUNKS, 4, STATE, WIDE), BF),
            pltpu.VMEM((CHUNKS, 2, STATE, WIDE), BF),
            pltpu.VMEM((CHUNKS, 4, STATE, WIDE), BF),
            pltpu.VMEM((CHUNKS, 5 * STATE, WIDE), BF),
            pltpu.VMEM((4, 8, SUB), F32),
            pltpu.VMEM((2, 8, SUB), F32),
            pltpu.VMEM((4, 8, SUB), F32),
            pltpu.VMEM((16, SUB), F32),
            pltpu.VMEM((CHUNKS, 16, WIDE), F32),
            dma((3,)), dma((3,)), dma((3,)), dma((3,)),
            dma((3,)), dma((3,)), dma(()), dma(()), dma((3,)), dma((3,)),
            dma((CHUNKS, 3)), dma((CHUNKS, 3)), dma((CHUNKS,)), dma((CHUNKS,)),
            dma((CHUNKS, 3)), dma((CHUNKS, 3)), dma((CHUNKS,)), dma((CHUNKS,)),
        ],
        compiler_params=pltpu.CompilerParams(
            collective_id=0, has_side_effects=True, vmem_limit_bytes=60 * 2**20
        ),
    )(
        mixer_input,
        write_map.T,
        read_map.T,
        step_size,
        log_decay,
        skip_gain.reshape(1, HEADS),
        level_table.T,
        level_index,
        jnp.asarray(range_matrix(), BF),
    )


def solution(mesh):
    placed = (
        P("seq", "head"),
        P("seq", "head"),
        P("seq", "head"),
        P("head", "seq"),
        P("head", "seq"),
        P("head"),
        P(),
        P(None, "seq"),
    )
    return jax.shard_map(
        on_device, mesh=mesh, in_specs=placed, out_specs=P("seq", "head"), check_vma=False
    )
```

time: 637 us -> 85.7 us (0.13); the launches traced: 628 us -> 84.9 us
  other arithmetic: 135 us -> 0 us
  local copies, waits for them, and re-layouts: 136 us -> 5.18 us
  blocking collectives: 101 us -> 0 us
  matrix products: 99.1 us -> 0 us
  waiting for transfers between devices: 84.9 us -> 0 us
  Pallas kernels: 0 us -> 79.7 us
  loops' own time: 58 us -> 0 us
  between operations: 13.7 us -> 0.01 us
    all_gather x3 -> x0, blocking collectives: 101 us -> none  [the longest x1 83.6 us: on_device(): lax.all_gather(own_total[None], 'seq', axis=0, tiled=True)]
    dot_general x32 -> x0, matrix products: 99.1 us -> none  [the longest x8 62.5 us: read_block(): jnp.einsum('tk,hkp->thp', queries, stacked, precision=lax.Precision.HIGHE...]
    while x56 -> x0, other arithmetic: 88.6 us -> none
    all_gather x1 -> x0, waiting for transfers between devices: 84.8 us -> none  [on_device(): lax.all_gather(own_state[None], 'seq', axis=0, tiled=True)]
    pallas_call x0 -> x1, Pallas kernels: none -> 79.7 us  [on_device(): pl.pallas_call(kernel, out_shape=jax.ShapeDtypeStruct((TOKENS, columns),...]
    another operation x2 -> x0, loops' own time: 58 us -> none  [the longest x1 39.8 us: on_device(): mixed = lax.map(read_block, block_ids)]
    dynamic_slice x100 -> x0, local copies, waits for them, and re-layouts: 54.3 us -> none  [the longest x32 25.9 us: block_rows(): return lax.dynamic_slice_in_dim(source, block_index * BLOCK, BLOCK, 0)]
    slice x16 -> x0, local copies, waits for them, and re-layouts: 44 us -> none  [the longest x4 36.9 us: pair_merge(): paired_state[:, 1]]
  transfers between devices with their start and end apart: 1 -> 0, of which waited for: 1 -> 0; matrix products, arithmetic and copies ran while one was open for 1% -> 0% of each run, Pallas kernels for 0% -> 0%
where the time goes in v1:
time: 85.7 us; the launch traced here: 84.9 us
  Pallas kernels  79.7 us (93%)
  local copies, waits for them, and re-layouts  5.18 us (6%)
    pallas_call x1, Pallas kernels, on_device(): pl.pallas_call(kernel, out_shape=jax.ShapeDtypeStruct((TOKENS, columns),...  79.7 us
    unnamed x1, local copies, waits for them, and re-layouts  5.18 us

profile of v1, /device:TPU:24, one launch (start us, length us, event | category | flops | bytes accessed | tf_op | source)
XLA Modules:
  0.0 84.9 jit_solution(17877512862970701751)
XLA Ops:
  0.0 79.7 %shard_map.91 = bf16[2048,1280]{1,0:T(8,128)(2,1)} custom-call(bf16[2048,1280]{1,0:T(8,128)(2,1)} %x_hbm.1, bf16[32,2048]{1,0:T(8,128)(2,1)} %bitcast.4, bf16[32,2048]{1,0:T(8,128)(2,1)} %bitcast.5, f32[20,2048]{1,0:T(8,128)} %step_in.1, f32[20,2048]{1,0:T(8,128)} %decay_in.1, f32[1,20]{1,0:T(1,128)} %bitcast.7, f32[8,9]{1,0:T(8,128)} %bitcast.6, ...), custom_call_target="tpu_custom_call" | custom-call | tf_op jit(solution)/shard_map/pallas_call | solution.py:512
  79.7 5.2 %copy.11 = bf16[2048,1280]{1,0:T(8,128)(2,1)} copy(bf16[2048,1280]{1,0:T(8,128)(2,1)} %shard_map.91) | data formatting | bytes 10485760

commit v2 on v1

--- a/solution.py
+++ b/solution.py
@@ -78,12 +78,12 @@
 
 
 def kernel(
-    x_hbm, b_own, c_own, step_in, decay_in, skip_in, table_in, index_in, ranges_in,
-    out_hbm,
-    x_s, b_t, c_t, ld_s, st_s, lw_s, tab_s, m_s, rv_s, colf, colhl, tots, tots3,
-    rexp, spread, tree, loc, scm, qs, part, out_s, zbuf, xbuf, ybuf, rbuf,
-    tz, tx, ty, secc, secw,
-    bs, br, cs, cr, tzs, tzr, txs, txr, tys, tyr, zs, zr, xs, xr, ys, yr, ins, outs,
+    x_hbm, b_own, c_own, step_in, decay_in, index_in, skip_in, table_in, ranges_in,
+    out_ref,
+    x_s, b_t, c_t, ld_in, st_in, ld_s, st_s, ix_s, lw_s, tab_s, m_s, m2_s, rv_s, colg, colhl, tots, tots3,
+    rexp, spread, take, lift, tree, loc, scm, qs, wide_s, decay_s, part, zbuf, xbuf, ybuf, rbuf,
+    tz, tx, ty, secc, secz, secw,
+    bs, br, cs, cr, tzs, tzr, txs, txr, tys, tyr, zs, zr, xs, xr, ys, yr, ins, small,
 ):
     seq = lax.axis_index("seq")
     me = lax.axis_index("head")
@@ -102,6 +102,20 @@
 
     def cols(j):
         return pl.ds(pl.multiple_of(j * SUB, SUB), SUB)
+
+    own_rows = pl.ds(pl.multiple_of(me * SHARE, SHARE), SHARE)
+    opp_rows = pl.ds(pl.multiple_of(opp * SHARE, SHARE), SHARE)
+    ld_s[16:32, :] = jnp.zeros((16, TOKENS), F32)
+    st_s[16:32, :] = jnp.zeros((16, TOKENS), F32)
+    inputs = [
+        pltpu.make_async_copy(b_own, b_t.at[own_rows], small.at[0]),
+        pltpu.make_async_copy(c_own, c_t.at[own_rows], small.at[1]),
+        pltpu.make_async_copy(decay_in, ld_in, small.at[2]),
+        pltpu.make_async_copy(step_in, st_in, small.at[3]),
+        pltpu.make_async_copy(index_in, ix_s, small.at[4]),
+    ]
+    for copy in inputs:
+        copy.start()
 
     peers = [at(h=sib), at(h=opp)]
     peers += [at(z=(z + d) % 4) for d in (1, 2, 3)]
@@ -119,10 +133,6 @@
     for c in range(CHUNKS):
         x_in(c).start()
 
-    own_rows = pl.ds(pl.multiple_of(me * SHARE, SHARE), SHARE)
-    opp_rows = pl.ds(pl.multiple_of(opp * SHARE, SHARE), SHARE)
-    b_t[own_rows, :] = b_own[...]
-    c_t[own_rows, :] = c_own[...]
 
     def share_copies(buf, ss, rs):
         own = buf.at[own_rows]
@@ -135,22 +145,21 @@
 
     b_copies = share_copies(b_t, bs, br)
     c_copies = share_copies(c_t, cs, cr)
+    inputs[0].wait()
     pl.semaphore_wait(barrier, len(peers))
     for k in (0, 1):
         b_copies[k].start()
-    for k in (0, 1):
-        c_copies[k].start()
-
-    ld_s[...] = jnp.zeros_like(ld_s)
-    st_s[...] = jnp.zeros_like(st_s)
-    ld_s[0:HEADS, :] = decay_in[...]
-    st_s[0:HEADS, :] = step_in[...]
+
+    for copy in inputs[2:]:
+        copy.wait()
+    ld_s[0:HEADS, :] = ld_in[...]
+    st_s[0:HEADS, :] = st_in[...]
     tab_s[...] = jnp.zeros_like(tab_s)
     tab_s[:, 0:LEVELS] = table_in[...]
     tab_t = tab_s[...].T
     lw_s[...] = jnp.ones_like(lw_s)
     weight = jnp.zeros((LEVELS, TOKENS), F32)
-    index = index_in[...]
+    index = ix_s[...]
     for e in range(TABLE):
         weight = weight + jnp.where(index == e, tab_t[0:LEVELS, e : e + 1], 0.0)
     lw_s[0:LEVELS, :] = weight
@@ -158,6 +167,8 @@
     lanes3 = lax.broadcasted_iota(jnp.int32, (3 * SUB, SUB), 1)
     rows3 = lax.broadcasted_iota(jnp.int32, (3 * SUB, SUB), 0) & (SUB - 1)
     upper = jnp.where(rows3 <= lanes3, 1.0, 0.0).astype(BF)
+
+    m2_s[...] = jnp.zeros_like(m2_s)
 
     def prepare(j, off):
         here = cols(j)
@@ -170,7 +181,10 @@
         rv = d2 - log_step
         for c in range(CHUNKS):
             rv_s[c, 0:4, here] = rv[4 * c : 4 * c + 4]
-        m_s[0:24, :] = d2 + jnp.log(lw[0:1]) * LOG2E
+        for n, piece in enumerate(split3(d2 + jnp.log(lw[0:1]) * LOG2E)):
+            m2_s[24 * n : 24 * n + 24, :] = piece.astype(F32)
+        colg[here, :] = m2_s[...].T.astype(BF)
+        m_s[0:24, :] = jnp.zeros((24, SUB), F32)
         m_s[20:21, :] = lw[8:9]
         m_s[COL_END : COL_END + 24, :] = jnp.exp2((total - d) * LOG2E + log_step)
         m_s[COL_OUT : COL_OUT + 24, :] = jnp.exp2(d2)
@@ -178,21 +192,29 @@
         m_s[COL_LEVEL : COL_LEVEL + 8, :] = lw[0:8]
         m_s[COL_SUM : COL_SUM + 24, :] = d
         mt = m_s[...].T
-        colf[here, :] = mt
         hi2, lo2 = split2(mt)
         colhl[here, 0:SUB] = hi2
         colhl[here, SUB : 2 * SUB] = lo2
         tots[pl.ds(j, 1), :] = mt[SUB - 1 : SUB, :]
         return off + total
 
-    lax.fori_loop(0, NSUB, prepare, jnp.zeros((24, SUB), F32))
+    lax.fori_loop(0, NSUB, prepare, jnp.zeros((24, SUB), F32), unroll=4)
 
     k_at = lax.broadcasted_iota(jnp.int32, (2 * SUB, WIDE), 0) & (SUB - 1)
     head_at = k_at - (lax.broadcasted_iota(jnp.int32, (2 * SUB, WIDE), 1) >> 6)
+
+    row_of = lax.broadcasted_iota(jnp.int32, (SUB, 4 * SUB), 0)
+    head_of = jnp.where(row_of < 24, row_of, jnp.where(row_of < 48, row_of - 24, row_of - 48))
+    head_of = jnp.where(row_of < 72, head_of, 4096)
+    taken = head_of - (lax.broadcasted_iota(jnp.int32, (SUB, 4 * SUB), 1) >> 7)
+    lane_in = lax.broadcasted_iota(jnp.int32, (2 * SUB, SUB), 0) & (SUB - 1)
+    for i, lane in enumerate(LEVEL_LANE):
+        lift[:, i * SUB : (i + 1) * SUB] = jnp.where(lane_in == lane, 1.0, 0.0).astype(BF)
 
     def build(c, carry):
         for g, base in enumerate(SPREAD_BASE):
             spread[g, c] = jnp.where(head_at == base + 4 * c, 1.0, 0.0).astype(BF)
+        take[c] = jnp.where(taken == 4 * c, 1.0, 0.0).astype(BF)
         return carry
 
     lax.fori_loop(0, CHUNKS, build, 0)
@@ -231,8 +253,9 @@
 
     b_copies[0].wait_recv()
     b_copies[2].start()
-    c_copies[0].wait_recv()
-    c_copies[2].start()
+    inputs[1].wait()
+    for k in (0, 1):
+        c_copies[k].start()
     b_copies[1].wait_recv()
     b_copies[2].wait_recv()
 
@@ -243,6 +266,13 @@
     tx_copy = remote(tx.at[xh], tx.at[xh], txs, txr, at(xh=1 - xh))
     tx_copy.start()
 
+    def ty_copy(d):
+        return remote(ty.at[y], ty.at[y], tys.at[d - 1], tyr.at[d - 1], at(y=(y + d) % 4))
+
+    def ty_arrival(d):
+        k = (y - d) % 4
+        return remote(ty.at[k], ty.at[k], tys.at[d - 1], tyr.at[d - 1], at(y=k))
+
     def z_copy(c, d):
         return remote(
             zbuf.at[c, z], zbuf.at[c, z], zs.at[c, d - 1], zr.at[c, d - 1], at(z=(z + d) % 4)
@@ -256,6 +286,15 @@
 
     def states(c, carry):
         x_in(c).wait()
+
+        @pl.when(c == 3)
+        def _():
+            c_copies[0].wait_recv()
+            c_copies[2].start()
+            tx_copy.wait_recv()
+            ty[y] = jnp.broadcast_to(tx[0, 0:1] + tx[1, 0:1], (8, SUB))
+            for d in (1, 2, 3):
+                ty_copy(d).start()
 
         def one(j, carry):
             here = cols(j)
@@ -264,7 +303,7 @@
             tree[j] = dot(b_t[:, here], scaled)
             return carry
 
-        lax.fori_loop(0, NSUB, one, 0)
+        lax.fori_loop(0, NSUB, one, 0, unroll=True)
         for i in range(4):
             for k in range(NSUB >> (i + 1)):
                 r = MERGE[i, k]
@@ -287,19 +326,6 @@
 
     lax.fori_loop(0, CHUNKS, states, 0)
 
-    tx_copy.wait_recv()
-    ty[y] = jnp.broadcast_to(tx[0, 0:1] + tx[1, 0:1], (8, SUB))
-
-    def ty_copy(d):
-        return remote(ty.at[y], ty.at[y], tys.at[d - 1], tyr.at[d - 1], at(y=(y + d) % 4))
-
-    def ty_arrival(d):
-        k = (y - d) % 4
-        return remote(ty.at[k], ty.at[k], tys.at[d - 1], tyr.at[d - 1], at(y=k))
-
-    for d in (1, 2, 3):
-        ty_copy(d).start()
-
     c_copies[1].wait_recv()
     c_copies[2].wait_recv()
     causal = lax.broadcasted_iota(jnp.int32, (SUB, SUB), 0) >= lax.broadcasted_iota(
@@ -310,50 +336,63 @@
         here = cols(j)
         c_rows = c_t[:, here].astype(F32).T
         scm[j] = jnp.where(causal, dot(c_rows.astype(BF), b_t[:, here]), 0.0)
-        tile = colf[here, :]
-        for i, lane in enumerate(LEVEL_LANE):
-            qs[here, i * STATE : (i + 1) * STATE] = (tile[:, lane : lane + 1] * c_rows).astype(BF)
+        level = dot(colhl[here, :], lift[...])
+        for i in range(LEVELS):
+            at_level = slice(i * STATE, (i + 1) * STATE)
+            qs[here, at_level] = (level[:, at_level] * c_rows).astype(BF)
         return carry
 
-    lax.fori_loop(0, NSUB, queries, 0)
-
-    for d in (1, 2, 3):
-        ty_arrival(d).wait_recv()
+    lax.fori_loop(0, NSUB, queries, 0, unroll=4)
 
     t0, t1, t2, t3 = far_t
-    u0, u1 = tx[0, 0:1], tx[1, 0:1]
-    v1, v2 = ty[1, 0:1], ty[2, 0:1]
 
     def only(flag, row):
         return jnp.where(flag, row, 0.0)
 
     run2 = only(z > 0, t0) + only(z > 1, t1) + only(z > 2, t2)
-    run3 = run2 + only(xh == 1, u0)
-    run4 = run3 + only(y == 3, v2)
     low_run = only(z == 3, t2)
     upper_z, upper_y = z >= 2, y >= 2
-    weights = [
-        jnp.exp(t1 + t2 + t3),
-        jnp.exp(t2 + t3),
-        jnp.exp(t3),
-        only(upper_z, jnp.exp(t1 + low_run)),
-        only(upper_z, jnp.exp(low_run)),
-        only(xh == 1, jnp.exp(run2)),
-        jnp.exp(u1),
-        jnp.exp(run3),
-        jnp.exp(v1 + run4),
-        jnp.exp(run4),
-    ]
+
+    def spread_weights(weights, where_to):
+        for n, w in enumerate(weights):
+            secc[n : n + 1, :] = w
+        compact = jnp.concatenate(split2(secc[...]), axis=1)
+
+        def spread_one(c, carry):
+            where_to[c] = dot(compact, spread[3, c])
+            return carry
+
+        lax.fori_loop(0, CHUNKS, spread_one, 0, unroll=True)
+
     secc[...] = jnp.zeros_like(secc)
-    for n, w in enumerate(weights):
-        secc[n : n + 1, :] = w
-    compact = jnp.concatenate(split2(secc[...]), axis=1)
-
-    def spread_weights(c, carry):
-        secw[c] = dot(compact, spread[3, c])
-        return carry
-
-    lax.fori_loop(0, CHUNKS, spread_weights, 0)
+    spread_weights(
+        [
+            jnp.exp(t1 + t2 + t3),
+            jnp.exp(t2 + t3),
+            jnp.exp(t3),
+            only(upper_z, jnp.exp(t1 + low_run)),
+            only(upper_z, jnp.exp(low_run)),
+        ],
+        secz,
+    )
+
+    def later_weights():
+        for d in (1, 2, 3):
+            ty_arrival(d).wait_recv()
+        u0, u1 = tx[0, 0:1], tx[1, 0:1]
+        v1, v2 = ty[1, 0:1], ty[2, 0:1]
+        run3 = run2 + only(xh == 1, u0)
+        run4 = run3 + only(y == 3, v2)
+        spread_weights(
+            [
+                only(xh == 1, jnp.exp(run2)),
+                jnp.exp(u1),
+                jnp.exp(run3),
+                jnp.exp(v1 + run4),
+                jnp.exp(run4),
+            ],
+            secw,
+        )
 
     def x_copy(c):
         return remote(xbuf.at[c, xh], xbuf.at[c, xh], xs.at[c], xr.at[c], at(xh=1 - xh))
@@ -374,7 +413,7 @@
     def after_z(c):
         for d in (1, 2, 3):
             z_arrival(c, d).wait_recv()
-        w = [secw[c, n : n + 1, :] for n in range(5)]
+        w = [secz[c, n : n + 1, :] for n in range(5)]
         s = [zbuf[c, k].astype(F32) for k in range(4)]
         xbuf[c, xh] = (w[0] * s[0] + w[1] * s[1] + (w[2] * s[2] + s[3])).astype(BF)
         x_copy(c).start()
@@ -386,14 +425,14 @@
     def after_x(c):
         x_arrival(c).wait_recv()
         s = [xbuf[c, k].astype(F32) for k in range(2)]
-        ybuf[c, y] = (secw[c, 6:7, :] * s[0] + s[1]).astype(BF)
+        ybuf[c, y] = (secw[c, 1:2, :] * s[0] + s[1]).astype(BF)
         for d in (1, 2, 3):
 
             @pl.when(y + d < 4)
             def _():
                 y_copy(c, d).start()
 
-        rbuf[c, 2 * STATE : 3 * STATE, :] = (secw[c, 5:6, :] * s[0]).astype(BF)
+        rbuf[c, 2 * STATE : 3 * STATE, :] = (secw[c, 0:1, :] * s[0]).astype(BF)
 
     def after_y(c):
         for d in (1, 2, 3):
@@ -402,19 +441,22 @@
             def _():
                 y_arrival(c, d).wait_recv()
 
-        near = secw[c, 7:8, :] * ybuf[c, jnp.maximum(y - 1, 0)].astype(F32)
+        near = secw[c, 2:3, :] * ybuf[c, jnp.maximum(y - 1, 0)].astype(F32)
         rbuf[c, 3 * STATE : 4 * STATE, :] = jnp.where(y % 2 == 1, near, 0.0).astype(BF)
-        wide = secw[c, 8:9, :] * ybuf[c, 0].astype(F32) + secw[c, 9:10, :] * ybuf[c, 1].astype(F32)
+        wide = secw[c, 3:4, :] * ybuf[c, 0].astype(F32) + secw[c, 4:5, :] * ybuf[c, 1].astype(F32)
         rbuf[c, 4 * STATE : 5 * STATE, :] = jnp.where(upper_y, wide, 0.0).astype(BF)
 
     low_half = lax.broadcasted_iota(jnp.int32, (SUB, SUB), 1) < 64
 
     def local_part(c):
-        turn = lax.rem(SUB - 4 * c, SUB)
         skip = rexp[c, SKIP_ROW : SKIP_ROW + 1, :]
         for j in range(NSUB):
             here = pl.ds(j * SUB, SUB)
-            tile = pltpu.roll(colf[here, :], turn, 1)
+            if j % (NSUB // 2) == 0:
+                many = pl.ds(j * SUB, TOKENS // 2)
+                wide_s[...] = dot(colg[many, :], take[c])
+                decay_s[...] = dot(colhl[many, :], spread[1, c])
+            now = pl.ds(j % (NSUB // 2) * SUB, SUB)
             masked = scm[j]
             xt = x_s[c, here, :]
             xf = xt.astype(F32)
@@ -422,7 +464,7 @@
             for pair in range(2):
                 mixes = []
                 for k in (2 * pair, 2 * pair + 1):
-                    gap = tile[:, k : k + 1] - rv_s[c, k : k + 1, here]
+                    gap = wide_s[now, k * SUB : (k + 1) * SUB] - rv_s[c, k : k + 1, here]
                     mixes.append((masked * jnp.exp2(jnp.minimum(gap, 64.0))).astype(BF))
                 xp = xf[:, pair * SUB : (pair + 1) * SUB]
                 both = jnp.concatenate(
@@ -439,38 +481,36 @@
                 q = jnp.concatenate([qs[here, i * STATE : (i + 1) * STATE] for i in bits], axis=1)
                 lo = LOCAL_AT[j, bits[0]] * STATE
                 near = dot(q, loc[c, lo : lo + len(bits) * STATE, :])
-                result = result + dot(colhl[here, :], spread[1, c]) * near
+                result = result + decay_s[now, :] * near
             part[c, here, :] = result
-
-    def out_copy(c):
-        return pltpu.make_async_copy(
-            out_s.at[c], out_hbm.at[:, pl.ds(pl.multiple_of(c * WIDE, WIDE), WIDE)], outs.at[c]
-        )
 
     def finish(c):
         def one(j, carry):
             here = pl.ds(pl.multiple_of(j * 256, 256), 256)
             far = dot(qs[here, 4 * STATE : 9 * STATE], rbuf[c])
             result = part[c, here, :] + dot(colhl[here, :], spread[2, c]) * far
-            out_s[c, here, :] = result.astype(BF)
+            out_ref[here, pl.ds(pl.multiple_of(c * WIDE, WIDE), WIDE)] = result.astype(BF)
             return carry
 
-        lax.fori_loop(0, TOKENS // 256, one, 0)
-        out_copy(c).start()
+        lax.fori_loop(0, TOKENS // 256, one, 0, unroll=True)
 
     def step(i, carry):
-        @pl.when(jnp.logical_and(i >= 1, i < 1 + CHUNKS))
+        @pl.when(i < CHUNKS)
         def _():
-            after_z(i - 1)
-
-        @pl.when(jnp.logical_and(i >= 3, i < 3 + CHUNKS))
+            after_z(i)
+
+        @pl.when(i == 1)
         def _():
-            after_x(i - 3)
-
-        @pl.when(i >= 5)
+            later_weights()
+
+        @pl.when(jnp.logical_and(i >= 2, i < 2 + CHUNKS))
         def _():
-            after_y(i - 5)
-            finish(i - 5)
+            after_x(i - 2)
+
+        @pl.when(i >= 4)
+        def _():
+            after_y(i - 4)
+            finish(i - 4)
 
         @pl.when(i < CHUNKS)
         def _():
@@ -478,7 +518,7 @@
 
         return carry
 
-    lax.fori_loop(0, 5 + CHUNKS, step, 0)
+    lax.fori_loop(0, 4 + CHUNKS, step, 0)
 
     for copies in (b_copies, c_copies):
         for copy in copies:
@@ -497,7 +537,6 @@
                 y_copy(c, d).wait_send()
 
         x_copy(c).wait_send()
-        out_copy(c).wait()
         return carry
 
     lax.fori_loop(0, CHUNKS, drain, 0)
@@ -511,31 +550,38 @@
     columns = HEADS * 64
     return pl.pallas_call(
         kernel,
-        out_shape=jax.ShapeDtypeStruct((TOKENS, columns), BF),
-        in_specs=[hbm] + [vmem] * 8,
-        out_specs=hbm,
+        out_shape=pltpu.VMEM((TOKENS, columns), BF),
+        in_specs=[hbm] * 6 + [vmem] * 3,
+        out_specs=vmem,
         scratch_shapes=[
             pltpu.VMEM((CHUNKS, TOKENS, WIDE), BF),
             pltpu.VMEM((STATE, TOKENS), BF),
             pltpu.VMEM((STATE, TOKENS), BF),
+            pltpu.VMEM((HEADS, TOKENS), F32),
+            pltpu.VMEM((HEADS, TOKENS), F32),
             pltpu.VMEM((32, TOKENS), F32),
             pltpu.VMEM((32, TOKENS), F32),
+            pltpu.VMEM((LEVELS, TOKENS), jnp.int32),
             pltpu.VMEM((16, TOKENS), F32),
             pltpu.VMEM((8, SUB), F32),
             pltpu.VMEM((SUB, SUB), F32),
+            pltpu.VMEM((SUB, SUB), F32),
             pltpu.VMEM((CHUNKS, 8, TOKENS), F32),
-            pltpu.VMEM((TOKENS, SUB), F32),
+            pltpu.VMEM((TOKENS, SUB), BF),
             pltpu.VMEM((TOKENS, 2 * SUB), BF),
             pltpu.VMEM((NSUB, SUB), F32),
             pltpu.VMEM((SUB, SUB), BF),
             pltpu.VMEM((CHUNKS, 64, WIDE), F32),
             pltpu.VMEM((4, CHUNKS, 2 * SUB, WIDE), BF),
+            pltpu.VMEM((CHUNKS, SUB, 4 * SUB), BF),
+            pltpu.VMEM((2 * SUB, LEVELS * SUB), BF),
             pltpu.VMEM((30, STATE, WIDE), F32),
             pltpu.VMEM((CHUNKS, len(LOCAL) * STATE, WIDE), BF),
             pltpu.VMEM((NSUB, SUB, SUB), F32),
             pltpu.VMEM((TOKENS, LEVELS * STATE), BF),
+            pltpu.VMEM((TOKENS // 2, 4 * SUB), F32),
+            pltpu.VMEM((TOKENS // 2, WIDE), F32),
             pltpu.VMEM((CHUNKS, TOKENS, WIDE), F32),
-            pltpu.VMEM((CHUNKS, TOKENS, WIDE), BF),
             pltpu.VMEM((CHUNKS, 4, STATE, WIDE), BF),
             pltpu.VMEM((CHUNKS, 2, STATE, WIDE), BF),
             pltpu.VMEM((CHUNKS, 4, STATE, WIDE), BF),
@@ -545,13 +591,14 @@
             pltpu.VMEM((4, 8, SUB), F32),
             pltpu.VMEM((16, SUB), F32),
             pltpu.VMEM((CHUNKS, 16, WIDE), F32),
+            pltpu.VMEM((CHUNKS, 16, WIDE), F32),
             dma((3,)), dma((3,)), dma((3,)), dma((3,)),
             dma((3,)), dma((3,)), dma(()), dma(()), dma((3,)), dma((3,)),
             dma((CHUNKS, 3)), dma((CHUNKS, 3)), dma((CHUNKS,)), dma((CHUNKS,)),
-            dma((CHUNKS, 3)), dma((CHUNKS, 3)), dma((CHUNKS,)), dma((CHUNKS,)),
+            dma((CHUNKS, 3)), dma((CHUNKS, 3)), dma((CHUNKS,)), dma((5,)),
         ],
         compiler_params=pltpu.CompilerParams(
-            collective_id=0, has_side_effects=True, vmem_limit_bytes=60 * 2**20
+            collective_id=0, has_side_effects=True, vmem_limit_bytes=54 * 2**20
         ),
     )(
         mixer_input,
@@ -559,9 +606,9 @@
         read_map.T,
         step_size,
         log_decay,
+        level_index,
         skip_gain.reshape(1, HEADS),
         level_table.T,
-        level_index,
         jnp.asarray(range_matrix(), BF),
     )
 

time: 85.7 us -> 47.1 us (0.55)
  Pallas kernels: 79.7 us -> 44.6 us
  local copies, waits for them, and re-layouts: 5.18 us -> 2.36 us
    pallas_call x1, Pallas kernels: 79.7 us -> 44.6 us  [on_device(): pl.pallas_call(kernel, out_shape=pltpu.VMEM((TOKENS, columns), BF), in_sp...]
    unnamed x1, local copies, waits for them, and re-layouts: 5.18 us -> 2.36 us
where the time goes in v2:
time: 47.1 us; the launch traced here: 46.9 us
  Pallas kernels  44.6 us (95%)
  local copies, waits for them, and re-layouts  2.36 us (5%)
    pallas_call x1, Pallas kernels, on_device(): pl.pallas_call(kernel, out_shape=pltpu.VMEM((TOKENS, columns), BF), in_sp...  44.6 us
    unnamed x1, local copies, waits for them, and re-layouts  2.36 us

profile of v2, /device:TPU:24, one launch (start us, length us, event | category | flops | bytes accessed | tf_op | source)
XLA Modules:
  0.0 46.9 jit_solution(6131818822370882249)
XLA Ops:
  0.0 44.6 %shard_map.91 = bf16[2048,1280]{1,0:T(8,128)(2,1)S(1)} custom-call(bf16[2048,1280]{1,0:T(8,128)(2,1)} %x_hbm.1, bf16[32,2048]{1,0:T(8,128)(2,1)} %bitcast.4, bf16[32,2048]{1,0:T(8,128)(2,1)} %bitcast.5, f32[20,2048]{1,0:T(8,128)} %step_in.1, f32[20,2048]{1,0:T(8,128)} %decay_in.1, s32[9,2048]{1,0:T(8,128)} %index_in.1, f32[1,20]{1,0:T(1,128)} %bitcast.7, ...), custom_call_target="tpu_custom_call" | custom-call | tf_op jit(solution)/shard_map/pallas_call | solution.py:551
  44.6 2.4 %copy.11 = bf16[2048,1280]{1,0:T(8,128)(2,1)} copy(bf16[2048,1280]{1,0:T(8,128)(2,1)S(1)} %shard_map.91) | data formatting | bytes 10485760

commit v3 on v2

--- a/solution.py
+++ b/solution.py
@@ -251,6 +251,16 @@
 
     lax.fori_loop(0, CHUNKS, spread_rows, 0)
 
+    def scale_inputs(c, carry):
+        x_in(c).wait()
+        for j in range(2):
+            here = pl.ds(j * TOKENS // 2, TOKENS // 2)
+            end = dot(colhl[here, :], spread[0, c])
+            part[c, here, :] = x_s[c, here, :].astype(F32) * end
+        return carry
+
+    lax.fori_loop(0, CHUNKS, scale_inputs, 0)
+
     b_copies[0].wait_recv()
     b_copies[2].start()
     inputs[1].wait()
@@ -285,8 +295,6 @@
     first = {0: 0, 1: 16, 2: 24, 3: 28}
 
     def states(c, carry):
-        x_in(c).wait()
-
         @pl.when(c == 3)
         def _():
             c_copies[0].wait_recv()
@@ -298,9 +306,7 @@
 
         def one(j, carry):
             here = cols(j)
-            end = dot(colhl[here, :], spread[0, c])
-            scaled = (x_s[c, here, :].astype(F32) * end).astype(BF)
-            tree[j] = dot(b_t[:, here], scaled)
+            tree[j] = dot(b_t[:, here], part[c, here, :].astype(BF))
             return carry
 
         lax.fori_loop(0, NSUB, one, 0, unroll=True)
@@ -486,13 +492,13 @@
 
     def finish(c):
         def one(j, carry):
-            here = pl.ds(pl.multiple_of(j * 256, 256), 256)
+            here = pl.ds(pl.multiple_of(j * 1024, 1024), 1024)
             far = dot(qs[here, 4 * STATE : 9 * STATE], rbuf[c])
             result = part[c, here, :] + dot(colhl[here, :], spread[2, c]) * far
             out_ref[here, pl.ds(pl.multiple_of(c * WIDE, WIDE), WIDE)] = result.astype(BF)
             return carry
 
-        lax.fori_loop(0, TOKENS // 256, one, 0, unroll=True)
+        lax.fori_loop(0, TOKENS // 1024, one, 0, unroll=True)
 
     def step(i, carry):
         @pl.when(i < CHUNKS)
@@ -507,14 +513,14 @@
         def _():
             after_x(i - 2)
 
+        @pl.when(i < CHUNKS)
+        def _():
+            local_part(i)
+
         @pl.when(i >= 4)
         def _():
             after_y(i - 4)
             finish(i - 4)
-
-        @pl.when(i < CHUNKS)
-        def _():
-            local_part(i)
 
         return carry
 

time: 47.1 us -> 46 us (0.977)
  Pallas kernels: 44.6 us -> 43.5 us
    pallas_call x1, Pallas kernels: 44.6 us -> 43.5 us  [on_device(): pl.pallas_call(kernel, out_shape=pltpu.VMEM((TOKENS, columns), BF), in_sp...]
where the time goes in v3:
time: 46 us; the launch traced here: 45.8 us
  Pallas kernels  43.5 us (95%)
  local copies, waits for them, and re-layouts  2.36 us (5%)
    pallas_call x1, Pallas kernels, on_device(): pl.pallas_call(kernel, out_shape=pltpu.VMEM((TOKENS, columns), BF), in_sp...  43.5 us
    unnamed x1, local copies, waits for them, and re-layouts  2.36 us

profile of v3, /device:TPU:24, one launch (start us, length us, event | category | flops | bytes accessed | tf_op | source)
XLA Modules:
  0.0 45.8 jit_solution(6434960804500202525)
XLA Ops:
  0.0 43.5 %shard_map.91 = bf16[2048,1280]{1,0:T(8,128)(2,1)S(1)} custom-call(bf16[2048,1280]{1,0:T(8,128)(2,1)} %x_hbm.1, bf16[32,2048]{1,0:T(8,128)(2,1)} %bitcast.4, bf16[32,2048]{1,0:T(8,128)(2,1)} %bitcast.5, f32[20,2048]{1,0:T(8,128)} %step_in.1, f32[20,2048]{1,0:T(8,128)} %decay_in.1, s32[9,2048]{1,0:T(8,128)} %index_in.1, f32[1,20]{1,0:T(1,128)} %bitcast.7, ...), custom_call_target="tpu_custom_call" | custom-call | tf_op jit(solution)/shard_map/pallas_call | solution.py:557
  43.5 2.4 %copy.11 = bf16[2048,1280]{1,0:T(8,128)(2,1)} copy(bf16[2048,1280]{1,0:T(8,128)(2,1)S(1)} %shard_map.91) | data formatting | bytes 10485760
